TPU v7x, 32 devices: a whole 2x2x4 slice. The times are simulated.
32 devices in a mesh: sy: 4 (over z), sx: 4 (over y, core), tp: 2 (over x).
Axes of the slice: x: 2, y: 2, z: 4, core: 2. Of those that a mesh axis runs over, the one named last changes fastest.
Arguments:
- features: bfloat16 [96, 64, 1408], P('sy', 'sx', 'tp'), may hold values from -6 to 6
- depth_kernel: float32 [7, 7, 1408], P(None, None, 'tp'), may hold values from -0.875 to 0.875
- depth_bias: float32 [1408], P('tp'), may hold values from -1 to 1
- norm_gain: float32 [1408], replicated, may hold values from 0.1 to 1.9
- norm_bias: float32 [1408], replicated, may hold values from -3 to 3
- up_weight: bfloat16 [1408, 5632], P(None, 'tp'), may hold values from -0.15625 to 0.15625
- up_bias: float32 [5632], P('tp'), may hold values from -3 to 3
- response_gain: float32 [5632], P('tp'), may hold values from -4 to 4
- response_shift: float32 [5632], P('tp'), may hold values from -3 to 3
- down_weight: bfloat16 [5632, 1408], P('tp', ('sy', 'sx')), may hold values from -0.078125 to 0.078125
- down_bias: float32 [1408], P('tp'), may hold values from -3 to 3
- tissue: int32 [12, 8], P('sy', 'sx'), may hold values from 0 to 1, as said below
- cotangent: bfloat16 [96, 64, 1408], P('sy', 'sx', 'tp'), may hold values from -6 to 6
Outputs:
- block_out: bfloat16 [96, 64, 1408], P('sy', 'sx', 'tp')
- feature_grad: bfloat16 [96, 64, 1408], P('sy', 'sx', 'tp')
Inputs may be any that keep to these rules, and one draw needn't show every extreme that they name: Each device's block of 3 x 2 tiles holds 1 to 4 tissue tiles; some device's block holds exactly 4.
All inputs are finite; a program needn't handle non-finite values.
Results may differ from a plain program's by a relative error of at most 0.0049.
The roundings to bfloat16 on the way count: a program that leaves them out, or rounds other values in their place, can miss the bound.
Values may be sent and summed in bfloat16 or wider, within the bound.
A program may use at most 128 MiB of HBM per device.

v0:
```python
import jax
import jax.numpy as jnp
from jax import lax
from jax.sharding import PartitionSpec as P

KERNEL = 7
TILE = 8
root_half = 0.7071067811865476
root_two_pi_inv = 0.3989422804014327


def extended(block, sides, width):
    for axis, dim in sides:
        count = lax.axis_size(axis)
        forward = [(i, i + 1) for i in range(count - 1)]
        backward = [(target, source) for source, target in forward]
        low = lax.ppermute(
            lax.slice_in_dim(block, block.shape[dim] - width, None, axis=dim), axis, forward
        )
        high = lax.ppermute(lax.slice_in_dim(block, 0, width, axis=dim), axis, backward)
        block = jnp.concatenate([low, block, high], axis=dim)
    return block


def gelu_value(values):
    return 0.5 * values * (1.0 + jax.scipy.special.erf(values * root_half))


def gelu_slope(values):
    return (
        0.5 * (1.0 + jax.scipy.special.erf(values * root_half))
        + values * jnp.exp(-0.5 * values * values) * root_two_pi_inv
    )


def depthwise(padded, kernel, rows_out, cols_out, flipped):
    summed = jnp.zeros((rows_out, cols_out, kernel.shape[2]), jnp.float32)
    last_tap = KERNEL - 1
    for row_tap in range(KERNEL):
        for col_tap in range(KERNEL):
            row_start = last_tap - row_tap if flipped else row_tap
            col_start = last_tap - col_tap if flipped else col_tap
            window = padded[row_start : row_start + rows_out, col_start : col_start + cols_out]
            summed = summed + window.astype(jnp.float32) * kernel[row_tap, col_tap]
    return summed


def extend(image):
    return extended(image, (("sy", 0), ("sx", 1)), KERNEL // 2)


def all_channels(rows_array):
    return lax.all_gather(rows_array, "tp", axis=1, tiled=True)


def global_vector(local_part):
    hidden_local = local_part.shape[0]
    placed = lax.dynamic_update_slice(
        jnp.zeros((hidden_local * lax.axis_size("tp"),), jnp.float32),
        local_part,
        (lax.axis_index("tp") * hidden_local,),
    )
    return lax.psum(placed, ("sy", "sx", "tp"))


def shards(
    features,
    depth_kernel,
    depth_bias,
    norm_gain,
    norm_bias,
    up_weight,
    up_bias,
    response_gain,
    response_shift,
    down_weight,
    down_bias,
    tissue,
    cotangent,
):
    image_rows, image_cols, local_channels = features.shape
    hidden_local = up_weight.shape[1]
    channel_start = lax.axis_index("tp") * local_channels
    contract_last = (((1,), (1,)), ((), ()))
    pixel_mask = jnp.repeat(jnp.repeat(tissue, TILE, axis=0), TILE, axis=1).astype(jnp.float32)
    mask_rows = pixel_mask.reshape(-1)

    def select(image):
        return image.reshape(image_rows * image_cols, image.shape[2])

    def restore(rows_array):
        return rows_array.reshape(image_rows, image_cols, rows_array.shape[1])

    convolved = (
        depthwise(extend(features), depth_kernel, image_rows, image_cols, False) + depth_bias
    ).astype(jnp.bfloat16)
    gathered = all_channels(select(convolved)).astype(jnp.float32)
    centre = jnp.mean(gathered, axis=1, keepdims=True)
    spread = jnp.mean(jnp.square(gathered - centre), axis=1, keepdims=True)
    inv_scale = lax.rsqrt(spread + 1e-06)
    standard = (gathered - centre) * inv_scale
    normed = (standard * norm_gain + norm_bias).astype(jnp.bfloat16)
    preact = jnp.dot(normed, up_weight, preferred_element_type=jnp.float32) + up_bias
    hidden = gelu_value(preact).astype(jnp.bfloat16)
    hidden_wide = hidden.astype(jnp.float32)
    squares = global_vector(jnp.sum(mask_rows[:, None] * hidden_wide * hidden_wide, axis=0))
    all_norms = jnp.sqrt(squares)
    norm_level = jnp.mean(all_norms) + 1e-06
    unit_start = lax.axis_index("tp") * hidden_local
    column_norms = lax.dynamic_slice_in_dim(all_norms, unit_start, hidden_local)
    norm_ratio = column_norms / norm_level
    response = (response_gain * hidden_wide * norm_ratio + response_shift + hidden_wide).astype(
        jnp.bfloat16
    )
    down_whole = lax.all_gather(down_weight, ("sy", "sx"), axis=1, tiled=True)
    partial_out = jnp.dot(response, down_whole, preferred_element_type=jnp.float32)
    branch = lax.psum_scatter(partial_out, "tp", scatter_dimension=1, tiled=True)
    branch_image = restore(branch + down_bias)
    block_out = (features.astype(jnp.float32) + pixel_mask[:, :, None] * branch_image).astype(
        jnp.bfloat16
    )
    masked_cot = (select(cotangent).astype(jnp.float32) * mask_rows[:, None]).astype(jnp.bfloat16)
    cot_wide = all_channels(masked_cot)
    back_hidden = lax.dot_general(
        cot_wide, down_whole, contract_last, preferred_element_type=jnp.float32
    )
    ratio_grad = global_vector(response_gain * jnp.sum(back_hidden * hidden_wide, axis=0))
    ratio_local = lax.dynamic_slice_in_dim(ratio_grad, unit_start, hidden_local)
    norms_grad = ratio_local / norm_level - jnp.sum(ratio_grad * all_norms) / (
        all_norms.shape[0] * norm_level * norm_level
    )
    hidden_grad = (
        back_hidden * (response_gain * norm_ratio + 1.0)
        + norms_grad * mask_rows[:, None] * hidden_wide / column_norms
    )
    preact_grad = (hidden_grad * gelu_slope(preact)).astype(jnp.bfloat16)
    grad_terms = lax.dot_general(
        preact_grad, up_weight, contract_last, preferred_element_type=jnp.float32
    )
    normed_grad = lax.psum(grad_terms, "tp")
    scaled = normed_grad * norm_gain
    convolved_grad = inv_scale * (
        scaled
        - jnp.mean(scaled, axis=1, keepdims=True)
        - standard * jnp.mean(scaled * standard, axis=1, keepdims=True)
    )
    convolved_grad = convolved_grad.astype(jnp.bfloat16)
    local_grad = lax.dynamic_slice_in_dim(convolved_grad, channel_start, local_channels, 1)
    grad_image = restore(local_grad)
    feature_grad = (
        cotangent.astype(jnp.float32)
        + depthwise(extend(grad_image), depth_kernel, image_rows, image_cols, True)
    ).astype(jnp.bfloat16)
    return (block_out, feature_grad)


def solution(mesh):
    placed = (
        P("sy", "sx", "tp"),
        P(None, None, "tp"),
        P("tp"),
        P(),
        P(),
        P(None, "tp"),
        P("tp"),
        P("tp"),
        P("tp"),
        P("tp", ("sy", "sx")),
        P("tp"),
        P("sy", "sx"),
        P("sy", "sx", "tp"),
    )
    return jax.shard_map(
        shards,
        mesh=mesh,
        in_specs=placed,
        out_specs=(P("sy", "sx", "tp"), P("sy", "sx", "tp")),
        check_vma=False,
    )
```

profile of v0, /device:TPU:0, one launch (start us, length us, event | category | flops | bytes accessed | tf_op | source)
XLA Modules:
  0.0 338.2 jit_solution(16324802515780690744)
XLA Ops:
  8.1 4.9 %collective-permute-start = (bf16[3,16,704]{2,1,0:T(8,128)(2,1)S(1)}, bf16[3,16,704]{2,1,0:T(8,128)(2,1)S(1)}, u32[]{:S(2)}, u32[]{:S(2)}) collective-permute-start(bf16[3,16,704]{2,1,0:T(8,128)(2,1)S(1)} %get-tuple-element.77), channel_id=1, source_target_pairs={{0,8},{8,16},{16,24},{1,9},{9,17},{17,25},{2,10},{10,18},{18,26},{... | collective-permute-start | bytes 202760 | tf_op jit(solution)/shard_map/ppermute | solution.py:17
  13.1 1.3 collective-permute-start.1
  14.4 1.4 slice_reduce_fusion.48
  15.8 1.1 slice_reduce_fusion.46
  16.9 1.2 constant_dynamic-update-slice_fusion.3
  18.2 1.2 collective-permute-done.1
  19.5 1.3 collective-permute-start.2
  20.8 1.3 collective-permute-start.3
  22.1 1.4 slice_reduce_fusion.47
  23.5 2.4 collective-permute-done.3
  25.9 14.1 %add_convert_fusion.2 = bf16[24,16,704]{2,1,0:T(8,128)(2,1)S(1)} fusion(bf16[24,16,704]{2,1,0:T(8,128)(2,1)S(1)} %copy-done, bf16[30,16,704]{2,1,0:T(8,128)(2,1)S(1)} %get-tuple-element.81, bf16[30,3,704]{2,1,0:T(4,128)(2,1)S(1)} %collective-permute-done.3, bf16[30,3,704]{2,1,0:T(4,128)(2,1)S(1)} %collective-permute-done.2, ...), kind=kLoop, calls=%fused_computation.149 | loop fusion | flops 74072064 | bytes 5395456 | tf_op jit(solution)/shard_map/convert_element_type | solution.py:96
  40.0 1.0 copy.21
  43.5 23.3 %all-gather.4.cloned.1.call-done = bf16[384,1408]{0,1:T(8,128)(2,1)} async-done(((bf16[384,704]{0,1:T(8,128)(2,1)}), bf16[384,1408]{0,1:T(8,128)(2,1)}) %all-gather.4.cloned.1.call-update) | async-done | bytes 1081360 | tf_op jit(solution)/shard_map/all_gather | solution.py:53
  66.7 1.7 copy.22
  69.2 8.6 %convolution_add_fusion = f32[384,2816]{1,0:T(8,128)} fusion(bf16[1408,2816]{1,0:T(8,128)(2,1)} %param.18, f32[2816]{0:T(1024)S(1)} %copy-done.7, f32[1408]{0:T(1024)S(1)} %copy-done.9, f32[1408]{0:T(1024)S(1)} %copy-done.3, bf16[384,1408]{1,0:T(8,128)(2,1)S(1)} %copy.22, f32[384]{0:T(512)S(1)} %add_rsqrt_fusion, f32[384]{0:T(512)S(1)} %broadcast_multiply_fusion.3), kind=kOutput, calls=%fused_computation.62 | convolution fusion | flops 3049390080 | bytes 13362176 | tf_op jit(solution)/shard_map/dot_general | solution.py:103
  77.8 12.8 %all-gather.8.cloned.1.call-done = bf16[384,1408]{0,1:T(8,128)(2,1)} async-done(((bf16[384,704]{0,1:T(8,128)(2,1)}), bf16[384,1408]{0,1:T(8,128)(2,1)}) %all-gather.8.cloned.1.call-update) | async-done | bytes 1081360 | tf_op jit(solution)/shard_map/all_gather | solution.py:53
  90.6 74.2 %all-gather.6.cloned.1.call-done = bf16[2816,1408]{0,1:T(8,128)(2,1)} async-done(((bf16[2816,88]{0,1:T(8,128)(2,1)}), bf16[2816,1408]{0,1:T(8,128)(2,1)}) %all-gather.6.cloned.1.call-update) | async-done | bytes 7929872 | tf_op jit(solution)/shard_map/all_gather | solution.py:115
  164.8 9.9 %fusion.10 = (f32[2816]{0:T(1024)S(1)}, f32[2816]{0:T(1024)S(1)}, bf16[384,2816]{1,0:T(8,128)(2,1)}, f32[384,2816]{1,0:T(8,128)}) fusion(f32[384]{0:T(512)S(1)} %convert_element_type.419, f32[384,2816]{1,0:T(8,128)} %convolution_add_fusion, bf16[384,1408]{0,1:T(8,128)(2,1)} %all-gather.8.cloned.1.call-done, bf16[2816,1408]{0,1:T(8,128)(2,1)} %all-gather.6.cloned.1.call-done), kind=kOutput, calls=%fused_computation.57 | convolution fusion | flops 3056953856 | bytes 19848704 | tf_op jit(solution)/shard_map/dot_general | solution.py:124
  175.2 39.6 %all-reduce = (f32[5632]{0:T(1024)S(1)}, f32[5632]{0:T(1024)S(1)}) all-reduce(f32[5632]{0:T(1024)S(1)} %dynamic_update_slice.6, f32[5632]{0:T(1024)S(1)} %multiply_dynamic-update-slice_fusion), channel_id=1, replica_groups=mesh['sy'=4,'sx'=4,'tp'=2] {'sy','sx','tp'}, use_global_device_ids=true, to_apply=%region_3.0 | all-reduce | flops 11264 | bytes 90112 | tf_op jit(solution)/shard_map/psum | solution.py:63
  216.7 12.4 %fusion.21 = f32[384,1408]{1,0:T(8,128)} fusion(bf16[1408,2816]{1,0:T(8,128)(2,1)} %param.18, f32[384,2816]{1,0:T(8,128)} %convolution_add_fusion, bf16[384,2816]{1,0:T(8,128)(2,1)} %get-tuple-element.63, f32[384,2816]{1,0:T(8,128)} %get-tuple-element.83, f32[2816]{0:T(1024)S(1)} %get-tuple-element.62, f32[2816]{0:T(1024)S(1)} %get-tuple-element.84, ...), kind=kOutput, calls=%fused_computation.74 | convolution fusion | flops 3062366208 | bytes 20941312 | tf_op jit(solution)/shard_map/dot_general | solution.py:137
  229.8 9.6 %fusion.16 = f32[384,1408]{0,1:T(8,128)} fusion(bf16[2816,1408]{0,1:T(8,128)(2,1)} %all-gather.6.cloned.1.call-done, bf16[384,2816]{1,0:T(8,128)(2,1)} %get-tuple-element.63, f32[2816]{0:T(1024)S(1)} %copy-done.8, f32[2816]{0:T(1024)S(1)} %get-tuple-element.61, f32[2816]{0:T(1024)S(1)} %copy-done.2), kind=kOutput, calls=%fused_computation.68 | convolution fusion | flops 3051552768 | bytes 12289024 | tf_op jit(solution)/shard_map/dot_general | solution.py:116
  239.4 54.7 %all-reduce.3.cloned.1.call-done = f32[384,1408]{1,0:T(8,128)} async-done(((f32[384,1408]{1,0:T(8,128)}), f32[384,1408]{1,0:T(8,128)}) %all-reduce.3.cloned.1.call-update) | async-done | bytes 2162704 | tf_op jit(solution)/shard_map/psum | solution.py:140
  294.1 2.3 fusion.102
  297.4 3.4 %collective-permute-start.4 = (bf16[3,16,704]{2,1,0:T(8,128)(2,1)S(1)}, bf16[3,16,704]{2,1,0:T(8,128)(2,1)S(1)}, u32[]{:S(2)}, u32[]{:S(2)}) collective-permute-start(bf16[3,16,704]{2,1,0:T(8,128)(2,1)S(1)} %bitcast.23), channel_id=1, source_target_pairs={{0,8},{8,16},{16,24},{1,9},{9,17},{17,25},{2,10},{10,18},{18,26},{... | collective-permute-start | bytes 202760 | tf_op jit(solution)/shard_map/ppermute | solution.py:17
  300.8 1.3 collective-permute-start.5
  302.7 4.3 %collective-permute-done.5 = bf16[3,16,704]{2,1,0:T(8,128)(2,1)S(1)} collective-permute-done((bf16[3,16,704]{2,1,0:T(8,128)(2,1)S(1)}, bf16[3,16,704]{2,1,0:T(8,128)(2,1)S(1)}, u32[]{:S(2)}, u32[]{:S(2)}) %collective-permute-start.5) | collective-permute-done | bytes 67616 | tf_op jit(solution)/shard_map/ppermute | solution.py:20
  307.2 1.3 collective-permute-start.6
  308.5 3.3 collective-permute-start.7
  313.1 10.3 %add_convert_fusion.1 = bf16[24,16,704]{2,1,0:T(8,128)(2,1)} fusion(bf16[24,16,704]{2,1,0:T(8,128)(2,1)S(1)} %bitcast.18, bf16[3,16,704]{2,1,0:T(8,128)(2,1)S(1)} %collective-permute-done.4, bf16[3,16,704]{2,1,0:T(8,128)(2,1)S(1)} %collective-permute-done.5, bf16[30,19,704]{2,1,0:T(8,128)(2,1)S(1)} %get-tuple-element.66, ...), kind=kLoop, calls=%fused_computation.148 | loop fusion | flops 41902080 | bytes 24603392 | tf_op jit(solution)/shard_map/convert_element_type | solution.py:153
  323.5 5.4 %reduce-scatter.2.cloned.1.call-done = f32[384,704]{0,1:T(8,128)} async-done(((f32[384,1408]{0,1:T(8,128)}), f32[384,704]{0,1:T(8,128)}) %reduce-scatter.2.cloned.1.call-update) | async-done | bytes 1081360 | tf_op jit(solution)/shard_map/reduce_scatter | solution.py:117
  328.9 1.4 broadcast_add_fusion
  330.7 1.0 fusion.48
  (66 shorter events, 9.6 us)
Async XLA Ops:
  7.2 59.6 %all-gather.4.cloned.1.call-start = ((), (), s32[]{:S(2)}) async-start(), calls=%async_computation.1 | async-start | bytes 1622016 | tf_op jit(solution)/shard_map/all_gather | solution.py:53
  8.1 8.8 %collective-permute-start = (bf16[3,16,704]{2,1,0:T(8,128)(2,1)S(1)}, bf16[3,16,704]{2,1,0:T(8,128)(2,1)S(1)}, u32[]{:S(2)}, u32[]{:S(2)}) collective-permute-start(bf16[3,16,704]{2,1,0:T(8,128)(2,1)S(1)} %get-tuple-element.77), channel_id=1, source_target_pairs={{0,8},{8,16},{16,24},{1,9},{9,17},{17,25},{2,10},{10,18},{18,26},{... | collective-permute-start | bytes 202760 | tf_op jit(solution)/shard_map/ppermute | solution.py:17
  13.1 6.2 %collective-permute-start.1 = (bf16[3,16,704]{2,1,0:T(8,128)(2,1)S(1)}, bf16[3,16,704]{2,1,0:T(8,128)(2,1)S(1)}, u32[]{:S(2)}, u32[]{:S(2)}) collective-permute-start(bf16[3,16,704]{2,1,0:T(8,128)(2,1)S(1)} %get-tuple-element.76), channel_id=1, source_target_pairs={{8,0},{16,8},{24,16},{9,1},{17,9},{25,17},{10,2},{18,10},{26,18},{... | collective-permute-start | bytes 202760 | tf_op jit(solution)/shard_map/ppermute | solution.py:20
  18.1 7.7 %copy-start = (bf16[24,16,704]{2,1,0:T(8,128)(2,1)S(1)}, bf16[24,16,704]{2,1,0:T(8,128)(2,1)}, u32[]{:S(2)}) copy-start(bf16[24,16,704]{2,1,0:T(8,128)(2,1)} %param.13) | copy-start | bytes 1622020
  18.1 7.7 %copy-start.5 = (f32[704]{0:T(1024)S(1)}, f32[704]{0:T(1024)}, u32[]{:S(2)}) copy-start(f32[704]{0:T(1024)} %param.15) | copy-start | bytes 8452
  19.5 4.0 %collective-permute-start.2 = (bf16[30,3,704]{2,1,0:T(4,128)(2,1)S(1)}, bf16[30,3,704]{2,1,0:T(4,128)(2,1)S(1)}, u32[]{:S(2)}, u32[]{:S(2)}) collective-permute-start(bf16[30,3,704]{2,1,0:T(4,128)(2,1)S(1)} %get-tuple-element.69), channel_id=1, source_target_pairs={{0,2},{2,4},{4,6},{1,3},{3,5},{5,7},{8,10},{10,12},{12,14},{9,11},... | collective-permute-start | bytes 380168 | tf_op jit(solution)/shard_map/ppermute | solution.py:17
  20.8 5.1 %collective-permute-start.3 = (bf16[30,3,704]{2,1,0:T(4,128)(2,1)S(1)}, bf16[30,3,704]{2,1,0:T(4,128)(2,1)S(1)}, u32[]{:S(2)}, u32[]{:S(2)}) collective-permute-start(bf16[30,3,704]{2,1,0:T(4,128)(2,1)S(1)} %get-tuple-element.70), channel_id=1, source_target_pairs={{2,0},{4,2},{6,4},{3,1},{5,3},{7,5},{10,8},{12,10},{14,12},{11,9},... | collective-permute-start | bytes 380168 | tf_op jit(solution)/shard_map/ppermute | solution.py:20
  40.0 1.1 copy-start.6
  40.0 1.6 copy-start.1
  41.0 49.5 %all-gather.8.cloned.1.call-start = ((), (), s32[]{:S(2)}) async-start(), calls=%async_computation.4 | async-start | bytes 1622016 | tf_op jit(solution)/shard_map/all_gather | solution.py:53
  42.7 122.1 %all-gather.6.cloned.1.call-start = ((), (), s32[]{:S(2)}) async-start(), calls=%async_computation.2 | async-start | bytes 8425472 | tf_op jit(solution)/shard_map/all_gather | solution.py:115
  43.4 250.7 %all-reduce.3.cloned.1.call-start = ((), (), s32[]{:S(2)}) async-start(), calls=%async_computation.5 | async-start | bytes 4325376 | tf_op jit(solution)/shard_map/psum | solution.py:140
  68.5 0.7 copy-start.3
  68.5 0.7 copy-start.7
  68.5 0.7 copy-start.9
  77.8 97.2 %copy-start.2 = (f32[2816]{0:T(1024)S(1)}, f32[2816]{0:T(1024)}, u32[]{:S(2)}) copy-start(f32[2816]{0:T(1024)} %param.20) | copy-start | bytes 33796
  229.1 0.7 copy-start.8
  229.1 99.8 %reduce-scatter.2.cloned.1.call-start = ((), (), s32[]{:S(2)}) async-start(), calls=%async_computation.3 | async-start | bytes 3244032 | tf_op jit(solution)/shard_map/reduce_scatter | solution.py:117
  297.4 5.4 %collective-permute-start.4 = (bf16[3,16,704]{2,1,0:T(8,128)(2,1)S(1)}, bf16[3,16,704]{2,1,0:T(8,128)(2,1)S(1)}, u32[]{:S(2)}, u32[]{:S(2)}) collective-permute-start(bf16[3,16,704]{2,1,0:T(8,128)(2,1)S(1)} %bitcast.23), channel_id=1, source_target_pairs={{0,8},{8,16},{16,24},{1,9},{9,17},{17,25},{2,10},{10,18},{18,26},{... | collective-permute-start | bytes 202760 | tf_op jit(solution)/shard_map/ppermute | solution.py:17
  300.8 6.2 %collective-permute-start.5 = (bf16[3,16,704]{2,1,0:T(8,128)(2,1)S(1)}, bf16[3,16,704]{2,1,0:T(8,128)(2,1)S(1)}, u32[]{:S(2)}, u32[]{:S(2)}) collective-permute-start(bf16[3,16,704]{2,1,0:T(8,128)(2,1)S(1)} %bitcast.22), channel_id=1, source_target_pairs={{8,0},{16,8},{24,16},{9,1},{17,9},{25,17},{10,2},{18,10},{26,18},{... | collective-permute-start | bytes 202760 | tf_op jit(solution)/shard_map/ppermute | solution.py:20
  307.2 4.7 %collective-permute-start.6 = (bf16[30,3,704]{2,1,0:T(4,128)(2,1)S(1)}, bf16[30,3,704]{2,1,0:T(4,128)(2,1)S(1)}, u32[]{:S(2)}, u32[]{:S(2)}) collective-permute-start(bf16[30,3,704]{2,1,0:T(4,128)(2,1)S(1)} %get-tuple-element.67), channel_id=1, source_target_pairs={{2,0},{4,2},{6,4},{3,1},{5,3},{7,5},{10,8},{12,10},{14,12},{11,9},... | collective-permute-start | bytes 380168 | tf_op jit(solution)/shard_map/ppermute | solution.py:20
  308.5 4.1 %collective-permute-start.7 = (bf16[30,3,704]{2,1,0:T(4,128)(2,1)S(1)}, bf16[30,3,704]{2,1,0:T(4,128)(2,1)S(1)}, u32[]{:S(2)}, u32[]{:S(2)}) collective-permute-start(bf16[30,3,704]{2,1,0:T(4,128)(2,1)S(1)} %get-tuple-element.68), channel_id=1, source_target_pairs={{0,2},{2,4},{4,6},{1,3},{3,5},{5,7},{8,10},{10,12},{12,14},{9,11},... | collective-permute-start | bytes 380168 | tf_op jit(solution)/shard_map/ppermute | solution.py:17
  313.1 15.8 %copy-start.4 = (f32[704]{0:T(1024)S(1)}, f32[704]{0:T(1024)}, u32[]{:S(2)}) copy-start(f32[704]{0:T(1024)} %param.23) | copy-start | bytes 8452
Sparse Core Ops, SparseCore 0:
  41.2 25.5 all-gather.3
  68.9 21.6 all-gather.7
  92.8 71.9 all-gather.5
  229.2 64.8 all-reduce.2
  296.3 32.5 reduce-scatter.1
where the time goes:
time: 339 us; the launch traced here: 338 us
  waiting for transfers between devices  180 us (53%)
  matrix products  40.4 us (12%)
  blocking collectives  39.6 us (12%)
  other arithmetic  33.2 us (10%)
  starting transfers between devices  18.3 us (5%)
  between operations  15.4 us (5%)
  local copies, waits for them, and re-layouts  11 us (3%)
    all_gather x1, waiting for transfers between devices, shards(): down_whole = lax.all_gather(down_weight, ('sy', 'sx'), axis=1, tiled=True)  74.2 us
    psum x1, waiting for transfers between devices, shards(): normed_grad = lax.psum(grad_terms, 'tp')  54.7 us
    psum x1, blocking collectives, global_vector(): return lax.psum(placed, ('sy', 'sx', 'tp'))  39.6 us
    all_gather x2, waiting for transfers between devices, all_channels(): return lax.all_gather(rows_array, 'tp', axis=1, tiled=True)  36 us
    convert_element_type x1, other arithmetic, shards(): convolved = (depthwise(extend(features), depth_kernel, image_rows, image_...  14.1 us
    ppermute x4, starting transfers between devices, extended(): lax.ppermute(lax.slice_in_dim(block, block.shape[dim] - width, None, axis...  12.9 us
    dot_general x1, matrix products, shards(): lax.dot_general(preact_grad, up_weight, contract_last, preferred_element_...  12.4 us
    convert_element_type x1, other arithmetic, shards(): feature_grad = (cotangent.astype(jnp.float32) + depthwise(extend(grad_ima...  10.3 us
  transfers between devices with their start and end apart: 13, of which 10 were waited for; matrix products, arithmetic and copies ran while one was open for 12% of the time, Pallas kernels for 0%

commit v1 on v0

--- a/solution.py
+++ b/solution.py
@@ -2,11 +2,20 @@
 import jax.numpy as jnp
 from jax import lax
 from jax.sharding import PartitionSpec as P
+from jax.lax import psum
 
 KERNEL = 7
 TILE = 8
 root_half = 0.7071067811865476
 root_two_pi_inv = 0.3989422804014327
+
+
+def render_terms_up(mine_x):
+    lane_axis = ("sx", "tp")
+    axis_tag = "sy"
+    for to_i in (axis_tag, lane_axis):
+        mine_x = psum(mine_x, to_i)
+    return mine_x
 
 
 def extended(block, sides, width):
@@ -60,7 +69,7 @@
         local_part,
         (lax.axis_index("tp") * hidden_local,),
     )
-    return lax.psum(placed, ("sy", "sx", "tp"))
+    return render_terms_up(placed)
 
 
 def shards(

time: 339 us -> 338 us (level)
  waiting for transfers between devices: 180 us -> 176 us
    psum x1, waiting for transfers between devices: 54.7 us -> 50.3 us  [shards(): normed_grad = lax.psum(grad_terms, 'tp')]
    psum x1 -> x2, blocking collectives: 39.6 us -> 42.3 us  [render_terms_up(): mine_x = psum(mine_x, to_i)]
  transfers between devices with their start and end apart: 13 -> 13, of which waited for: 10 -> 10; matrix products, arithmetic and copies ran while one was open for 12% -> 13% of each run, Pallas kernels for 0% -> 0%
where the time goes in v1:
time: 338 us; the launch traced here: 337 us
  waiting for transfers between devices  176 us (52%)
  blocking collectives  42.3 us (13%)
  matrix products  41.2 us (12%)
  other arithmetic  33.2 us (10%)
  starting transfers between devices  18 us (5%)
  between operations  15.4 us (5%)
  local copies, waits for them, and re-layouts  11.1 us (3%)
    all_gather x1, waiting for transfers between devices, shards(): down_whole = lax.all_gather(down_weight, ('sy', 'sx'), axis=1, tiled=True)  74.2 us
    psum x1, waiting for transfers between devices, shards(): normed_grad = lax.psum(grad_terms, 'tp')  50.3 us
    psum x2, blocking collectives, render_terms_up(): mine_x = psum(mine_x, to_i)  42.3 us
    all_gather x2, waiting for transfers between devices, all_channels(): return lax.all_gather(rows_array, 'tp', axis=1, tiled=True)  36 us
    convert_element_type x1, other arithmetic, shards(): convolved = (depthwise(extend(features), depth_kernel, image_rows, image_...  14.1 us
    ppermute x4, starting transfers between devices, extended(): lax.ppermute(lax.slice_in_dim(block, block.shape[dim] - width, None, axis...  12.7 us
    dot_general x1, matrix products, shards(): lax.dot_general(preact_grad, up_weight, contract_last, preferred_element_...  12.4 us
    convert_element_type x1, other arithmetic, shards(): feature_grad = (cotangent.astype(jnp.float32) + depthwise(extend(grad_ima...  10.3 us
  transfers between devices with their start and end apart: 13, of which 10 were waited for; matrix products, arithmetic and copies ran while one was open for 13% of the time, Pallas kernels for 0%

profile of v1, /device:TPU:0, one launch (start us, length us, event | category | flops | bytes accessed | tf_op | source)
XLA Modules:
  0.0 337.4 jit_solution(18162666066133131755)
XLA Ops:
  8.1 4.9 %collective-permute-start = (bf16[3,16,704]{2,1,0:T(8,128)(2,1)S(1)}, bf16[3,16,704]{2,1,0:T(8,128)(2,1)S(1)}, u32[]{:S(2)}, u32[]{:S(2)}) collective-permute-start(bf16[3,16,704]{2,1,0:T(8,128)(2,1)S(1)} %get-tuple-element.79), channel_id=1, source_target_pairs={{0,8},{8,16},{16,24},{1,9},{9,17},{17,25},{2,10},{10,18},{18,26},{... | collective-permute-start | bytes 202760 | tf_op jit(solution)/shard_map/ppermute | solution.py:26
  13.1 1.3 collective-permute-start.1
  14.4 1.4 slice_reduce_fusion.48
  15.8 1.1 slice_reduce_fusion.46
  16.9 1.2 constant_dynamic-update-slice_fusion.3
  18.2 1.2 collective-permute-done.1
  19.5 1.3 collective-permute-start.2
  20.8 1.3 collective-permute-start.3
  22.1 1.4 slice_reduce_fusion.47
  23.5 2.4 collective-permute-done.3
  25.9 14.1 %add_convert_fusion.2 = bf16[24,16,704]{2,1,0:T(8,128)(2,1)S(1)} fusion(bf16[24,16,704]{2,1,0:T(8,128)(2,1)S(1)} %copy-done, bf16[30,16,704]{2,1,0:T(8,128)(2,1)S(1)} %get-tuple-element.83, bf16[30,3,704]{2,1,0:T(4,128)(2,1)S(1)} %collective-permute-done.3, bf16[30,3,704]{2,1,0:T(4,128)(2,1)S(1)} %collective-permute-done.2, ...), kind=kLoop, calls=%fused_computation.149 | loop fusion | flops 74072064 | bytes 5395456 | tf_op jit(solution)/shard_map/convert_element_type | solution.py:105
  40.0 1.0 copy.21
  43.5 23.3 %all-gather.4.cloned.1.call-done = bf16[384,1408]{0,1:T(8,128)(2,1)} async-done(((bf16[384,704]{0,1:T(8,128)(2,1)}), bf16[384,1408]{0,1:T(8,128)(2,1)}) %all-gather.4.cloned.1.call-update) | async-done | bytes 1081360 | tf_op jit(solution)/shard_map/all_gather | solution.py:62
  66.7 1.7 copy.22
  69.2 8.6 %convolution_add_fusion = f32[384,2816]{1,0:T(8,128)} fusion(bf16[1408,2816]{1,0:T(8,128)(2,1)} %param.18, f32[2816]{0:T(1024)S(1)} %copy-done.7, f32[1408]{0:T(1024)S(1)} %copy-done.9, f32[1408]{0:T(1024)S(1)} %copy-done.3, bf16[384,1408]{1,0:T(8,128)(2,1)S(1)} %copy.22, f32[384]{0:T(512)S(1)} %add_rsqrt_fusion, f32[384]{0:T(512)S(1)} %broadcast_multiply_fusion.3), kind=kOutput, calls=%fused_computation.62 | convolution fusion | flops 3049390080 | bytes 13362176 | tf_op jit(solution)/shard_map/dot_general | solution.py:112
  77.8 12.8 %all-gather.8.cloned.1.call-done = bf16[384,1408]{0,1:T(8,128)(2,1)} async-done(((bf16[384,704]{0,1:T(8,128)(2,1)}), bf16[384,1408]{0,1:T(8,128)(2,1)}) %all-gather.8.cloned.1.call-update) | async-done | bytes 1081360 | tf_op jit(solution)/shard_map/all_gather | solution.py:62
  90.6 74.2 %all-gather.6.cloned.1.call-done = bf16[2816,1408]{0,1:T(8,128)(2,1)} async-done(((bf16[2816,88]{0,1:T(8,128)(2,1)}), bf16[2816,1408]{0,1:T(8,128)(2,1)}) %all-gather.6.cloned.1.call-update) | async-done | bytes 7929872 | tf_op jit(solution)/shard_map/all_gather | solution.py:124
  164.8 9.9 %fusion.10 = (f32[2816]{0:T(1024)S(1)}, f32[2816]{0:T(1024)S(1)}, bf16[384,2816]{1,0:T(8,128)(2,1)}, f32[384,2816]{1,0:T(8,128)}) fusion(f32[384]{0:T(512)S(1)} %convert_element_type.419, f32[384,2816]{1,0:T(8,128)} %convolution_add_fusion, bf16[384,1408]{0,1:T(8,128)(2,1)} %all-gather.8.cloned.1.call-done, bf16[2816,1408]{0,1:T(8,128)(2,1)} %all-gather.6.cloned.1.call-done), kind=kOutput, calls=%fused_computation.57 | convolution fusion | flops 3056953856 | bytes 19848704 | tf_op jit(solution)/shard_map/dot_general | solution.py:133
  175.2 17.8 %all-reduce.1 = (f32[5632]{0:T(1024)S(1)}, f32[5632]{0:T(1024)S(1)}) all-reduce(f32[5632]{0:T(1024)S(1)} %dynamic_update_slice.6, f32[5632]{0:T(1024)S(1)} %multiply_dynamic-update-slice_fusion), channel_id=1, replica_groups=mesh['sy'=4,'sx'=4,'tp'=2] {'sy'}, use_global_device_ids=true, to_apply=%region_3.0 | all-reduce | flops 11264 | bytes 90112 | tf_op jit(solution)/shard_map/psum | solution.py:17
  192.9 24.5 %all-reduce = (f32[5632]{0:T(1024)S(1)}, f32[5632]{0:T(1024)S(1)}) all-reduce(f32[5632]{0:T(1024)S(1)} %get-tuple-element.59, f32[5632]{0:T(1024)S(1)} %get-tuple-element.60), channel_id=1, replica_groups=mesh['sy'=4,'sx'=4,'tp'=2] {'sx','tp'}, use_global_device_ids=true, to_apply=%region_4.0 | all-reduce | flops 11264 | bytes 90112 | tf_op jit(solution)/shard_map/psum | solution.py:17
  219.5 12.4 %fusion.21 = f32[384,1408]{1,0:T(8,128)} fusion(bf16[1408,2816]{1,0:T(8,128)(2,1)} %param.18, f32[384,2816]{1,0:T(8,128)} %convolution_add_fusion, bf16[384,2816]{1,0:T(8,128)(2,1)} %get-tuple-element.65, f32[384,2816]{1,0:T(8,128)} %get-tuple-element.85, f32[2816]{0:T(1024)S(1)} %get-tuple-element.64, f32[2816]{0:T(1024)S(1)} %get-tuple-element.86, ...), kind=kOutput, calls=%fused_computation.74 | convolution fusion | flops 3062366208 | bytes 20941312 | tf_op jit(solution)/shard_map/dot_general | solution.py:146
  232.6 10.3 %fusion.16 = f32[384,1408]{0,1:T(8,128)} fusion(bf16[2816,1408]{0,1:T(8,128)(2,1)} %all-gather.6.cloned.1.call-done, bf16[384,2816]{1,0:T(8,128)(2,1)} %get-tuple-element.65, f32[2816]{0:T(1024)S(1)} %copy-done.8, f32[2816]{0:T(1024)S(1)} %get-tuple-element.63, f32[2816]{0:T(1024)S(1)} %copy-done.2), kind=kOutput, calls=%fused_computation.68 | convolution fusion | flops 3051552768 | bytes 12289024 | tf_op jit(solution)/shard_map/dot_general | solution.py:125
  242.9 50.3 %all-reduce.4.cloned.1.call-done = f32[384,1408]{1,0:T(8,128)} async-done(((f32[384,1408]{1,0:T(8,128)}), f32[384,1408]{1,0:T(8,128)}) %all-reduce.4.cloned.1.call-update) | async-done | bytes 2162704 | tf_op jit(solution)/shard_map/psum | solution.py:149
  293.2 2.2 fusion.102
  296.5 3.4 %collective-permute-start.4 = (bf16[3,16,704]{2,1,0:T(8,128)(2,1)S(1)}, bf16[3,16,704]{2,1,0:T(8,128)(2,1)S(1)}, u32[]{:S(2)}, u32[]{:S(2)}) collective-permute-start(bf16[3,16,704]{2,1,0:T(8,128)(2,1)S(1)} %bitcast.23), channel_id=1, source_target_pairs={{0,8},{8,16},{16,24},{1,9},{9,17},{17,25},{2,10},{10,18},{18,26},{... | collective-permute-start | bytes 202760 | tf_op jit(solution)/shard_map/ppermute | solution.py:26
  299.9 1.3 collective-permute-start.5
  301.8 4.3 %collective-permute-done.5 = bf16[3,16,704]{2,1,0:T(8,128)(2,1)S(1)} collective-permute-done((bf16[3,16,704]{2,1,0:T(8,128)(2,1)S(1)}, bf16[3,16,704]{2,1,0:T(8,128)(2,1)S(1)}, u32[]{:S(2)}, u32[]{:S(2)}) %collective-permute-start.5) | collective-permute-done | bytes 67616 | tf_op jit(solution)/shard_map/ppermute | solution.py:29
  306.3 1.3 collective-permute-start.6
  307.6 3.0 collective-permute-start.7
  312.2 10.3 %add_convert_fusion.1 = bf16[24,16,704]{2,1,0:T(8,128)(2,1)} fusion(bf16[24,16,704]{2,1,0:T(8,128)(2,1)S(1)} %bitcast.18, bf16[3,16,704]{2,1,0:T(8,128)(2,1)S(1)} %collective-permute-done.4, bf16[3,16,704]{2,1,0:T(8,128)(2,1)S(1)} %collective-permute-done.5, bf16[30,19,704]{2,1,0:T(8,128)(2,1)S(1)} %get-tuple-element.68, ...), kind=kLoop, calls=%fused_computation.148 | loop fusion | flops 41902080 | bytes 24603392 | tf_op jit(solution)/shard_map/convert_element_type | solution.py:162
  322.6 5.4 %reduce-scatter.2.cloned.1.call-done = f32[384,704]{0,1:T(8,128)} async-done(((f32[384,1408]{0,1:T(8,128)}), f32[384,704]{0,1:T(8,128)}) %reduce-scatter.2.cloned.1.call-update) | async-done | bytes 1081360 | tf_op jit(solution)/shard_map/reduce_scatter | solution.py:126
  328.0 1.4 broadcast_add_fusion
  (67 shorter events, 10.9 us)
Async XLA Ops:
  7.2 59.6 %all-gather.4.cloned.1.call-start = ((), (), s32[]{:S(2)}) async-start(), calls=%async_computation.1 | async-start | bytes 1622016 | tf_op jit(solution)/shard_map/all_gather | solution.py:62
  8.1 8.8 %collective-permute-start = (bf16[3,16,704]{2,1,0:T(8,128)(2,1)S(1)}, bf16[3,16,704]{2,1,0:T(8,128)(2,1)S(1)}, u32[]{:S(2)}, u32[]{:S(2)}) collective-permute-start(bf16[3,16,704]{2,1,0:T(8,128)(2,1)S(1)} %get-tuple-element.79), channel_id=1, source_target_pairs={{0,8},{8,16},{16,24},{1,9},{9,17},{17,25},{2,10},{10,18},{18,26},{... | collective-permute-start | bytes 202760 | tf_op jit(solution)/shard_map/ppermute | solution.py:26
  13.1 6.2 %collective-permute-start.1 = (bf16[3,16,704]{2,1,0:T(8,128)(2,1)S(1)}, bf16[3,16,704]{2,1,0:T(8,128)(2,1)S(1)}, u32[]{:S(2)}, u32[]{:S(2)}) collective-permute-start(bf16[3,16,704]{2,1,0:T(8,128)(2,1)S(1)} %get-tuple-element.78), channel_id=1, source_target_pairs={{8,0},{16,8},{24,16},{9,1},{17,9},{25,17},{10,2},{18,10},{26,18},{... | collective-permute-start | bytes 202760 | tf_op jit(solution)/shard_map/ppermute | solution.py:29
  18.1 7.7 %copy-start = (bf16[24,16,704]{2,1,0:T(8,128)(2,1)S(1)}, bf16[24,16,704]{2,1,0:T(8,128)(2,1)}, u32[]{:S(2)}) copy-start(bf16[24,16,704]{2,1,0:T(8,128)(2,1)} %param.13) | copy-start | bytes 1622020
  18.1 7.7 %copy-start.5 = (f32[704]{0:T(1024)S(1)}, f32[704]{0:T(1024)}, u32[]{:S(2)}) copy-start(f32[704]{0:T(1024)} %param.15) | copy-start | bytes 8452
  19.5 4.0 %collective-permute-start.2 = (bf16[30,3,704]{2,1,0:T(4,128)(2,1)S(1)}, bf16[30,3,704]{2,1,0:T(4,128)(2,1)S(1)}, u32[]{:S(2)}, u32[]{:S(2)}) collective-permute-start(bf16[30,3,704]{2,1,0:T(4,128)(2,1)S(1)} %get-tuple-element.71), channel_id=1, source_target_pairs={{0,2},{2,4},{4,6},{1,3},{3,5},{5,7},{8,10},{10,12},{12,14},{9,11},... | collective-permute-start | bytes 380168 | tf_op jit(solution)/shard_map/ppermute | solution.py:26
  20.8 5.1 %collective-permute-start.3 = (bf16[30,3,704]{2,1,0:T(4,128)(2,1)S(1)}, bf16[30,3,704]{2,1,0:T(4,128)(2,1)S(1)}, u32[]{:S(2)}, u32[]{:S(2)}) collective-permute-start(bf16[30,3,704]{2,1,0:T(4,128)(2,1)S(1)} %get-tuple-element.72), channel_id=1, source_target_pairs={{2,0},{4,2},{6,4},{3,1},{5,3},{7,5},{10,8},{12,10},{14,12},{11,9},... | collective-permute-start | bytes 380168 | tf_op jit(solution)/shard_map/ppermute | solution.py:29
  40.0 1.1 copy-start.6
  40.0 1.6 copy-start.1
  41.0 49.5 %all-gather.8.cloned.1.call-start = ((), (), s32[]{:S(2)}) async-start(), calls=%async_computation.4 | async-start | bytes 1622016 | tf_op jit(solution)/shard_map/all_gather | solution.py:62
  42.7 122.1 %all-gather.6.cloned.1.call-start = ((), (), s32[]{:S(2)}) async-start(), calls=%async_computation.2 | async-start | bytes 8425472 | tf_op jit(solution)/shard_map/all_gather | solution.py:124
  43.4 249.8 %all-reduce.4.cloned.1.call-start = ((), (), s32[]{:S(2)}) async-start(), calls=%async_computation.5 | async-start | bytes 4325376 | tf_op jit(solution)/shard_map/psum | solution.py:149
  68.5 0.7 copy-start.3
  68.5 0.7 copy-start.7
  68.5 0.7 copy-start.9
  77.8 97.2 %copy-start.2 = (f32[2816]{0:T(1024)S(1)}, f32[2816]{0:T(1024)}, u32[]{:S(2)}) copy-start(f32[2816]{0:T(1024)} %param.20) | copy-start | bytes 33796
  231.9 0.7 copy-start.8
  231.9 96.1 %reduce-scatter.2.cloned.1.call-start = ((), (), s32[]{:S(2)}) async-start(), calls=%async_computation.3 | async-start | bytes 3244032 | tf_op jit(solution)/shard_map/reduce_scatter | solution.py:126
  296.5 5.4 %collective-permute-start.4 = (bf16[3,16,704]{2,1,0:T(8,128)(2,1)S(1)}, bf16[3,16,704]{2,1,0:T(8,128)(2,1)S(1)}, u32[]{:S(2)}, u32[]{:S(2)}) collective-permute-start(bf16[3,16,704]{2,1,0:T(8,128)(2,1)S(1)} %bitcast.23), channel_id=1, source_target_pairs={{0,8},{8,16},{16,24},{1,9},{9,17},{17,25},{2,10},{10,18},{18,26},{... | collective-permute-start | bytes 202760 | tf_op jit(solution)/shard_map/ppermute | solution.py:26
  299.9 6.2 %collective-permute-start.5 = (bf16[3,16,704]{2,1,0:T(8,128)(2,1)S(1)}, bf16[3,16,704]{2,1,0:T(8,128)(2,1)S(1)}, u32[]{:S(2)}, u32[]{:S(2)}) collective-permute-start(bf16[3,16,704]{2,1,0:T(8,128)(2,1)S(1)} %bitcast.22), channel_id=1, source_target_pairs={{8,0},{16,8},{24,16},{9,1},{17,9},{25,17},{10,2},{18,10},{26,18},{... | collective-permute-start | bytes 202760 | tf_op jit(solution)/shard_map/ppermute | solution.py:29
  306.3 4.4 %collective-permute-start.6 = (bf16[30,3,704]{2,1,0:T(4,128)(2,1)S(1)}, bf16[30,3,704]{2,1,0:T(4,128)(2,1)S(1)}, u32[]{:S(2)}, u32[]{:S(2)}) collective-permute-start(bf16[30,3,704]{2,1,0:T(4,128)(2,1)S(1)} %get-tuple-element.69), channel_id=1, source_target_pairs={{2,0},{4,2},{6,4},{3,1},{5,3},{7,5},{10,8},{12,10},{14,12},{11,9},... | collective-permute-start | bytes 380168 | tf_op jit(solution)/shard_map/ppermute | solution.py:29
  307.6 4.1 %collective-permute-start.7 = (bf16[30,3,704]{2,1,0:T(4,128)(2,1)S(1)}, bf16[30,3,704]{2,1,0:T(4,128)(2,1)S(1)}, u32[]{:S(2)}, u32[]{:S(2)}) collective-permute-start(bf16[30,3,704]{2,1,0:T(4,128)(2,1)S(1)} %get-tuple-element.70), channel_id=1, source_target_pairs={{0,2},{2,4},{4,6},{1,3},{3,5},{5,7},{8,10},{10,12},{12,14},{9,11},... | collective-permute-start | bytes 380168 | tf_op jit(solution)/shard_map/ppermute | solution.py:26
  312.2 15.8 %copy-start.4 = (f32[704]{0:T(1024)S(1)}, f32[704]{0:T(1024)}, u32[]{:S(2)}) copy-start(f32[704]{0:T(1024)} %param.23) | copy-start | bytes 8452
Sparse Core Ops, SparseCore 0:
  41.2 25.5 all-gather.3
  68.9 21.6 all-gather.7
  92.8 71.9 all-gather.5
  232.0 61.1 all-reduce.3
  295.4 32.5 reduce-scatter.1
